TPU v7x, 512 devices: a whole 4x4x16 slice. The times are simulated.
512 devices in a mesh: tok: 2 (over core), head: 16 (over y, x), exp: 16 (over z).
Axes of the slice: x: 4, y: 4, z: 16, core: 2. Of those that a mesh axis runs over, the one named last changes fastest.
Arguments:
- context: bfloat16 [16, 64, 4096], P('exp', 'tok', 'head'), may hold values from -6 to 6
- out_proj: bfloat16 [4096, 4096], P('head', 'exp'), may hold values from -0.125 to 0.125
- stream: float32 [16, 64, 4096], P('exp', 'tok', 'head'), may hold values from -75 to 75
- norm_gain: float32 [4096], replicated, may hold values from 0.1 to 1.9
- expert_ids: int32 [16, 64, 8], P('exp', 'tok'), may hold values from 0 to 31, as said below
- slot_ids: int32 [16, 64, 8], P('exp', 'tok'), may hold values from -1 to 11, as said below
- gate_probs: float32 [16, 64, 8], P('exp', 'tok'), may hold values from 0.02 to 0.3
- w_gate: bfloat16 [32, 3072, 4096], P(('tok', 'exp'), 'head'), may hold values from -0.09375 to 0.09375
- w_up: bfloat16 [32, 3072, 4096], P(('tok', 'exp'), 'head'), may hold values from -0.09375 to 0.09375
- w_down: bfloat16 [32, 3072, 4096], P(('tok', 'exp'), 'head'), may hold values from -0.15625 to 0.15625
Outputs:
- mixed: float32 [16, 64, 4096], P('exp', 'tok', 'head')
Inputs may be any that keep to these rules, and one draw needn't show every extreme that they name: `expert_ids`: each token names 8 different experts. `slot_ids`: within a block of 32 consecutive tokens of one image, the choices of one expert take slots 0, 1, 2, ... in token order until its 12 slots are full, later ones get -1; in every block some expert fills all 12 slots.
All inputs are finite; a program needn't handle non-finite values.
Results may differ from a plain program's by a relative error of at most 0.0034.
Values may be sent and summed in bfloat16 or wider, within the bound.
No kernel may reach another device: no remote copies, remote signals or barrier semaphores. Data moves between devices by JAX's collectives and lax.ppermute only.
A program may use at most 64 MiB of HBM per device.

v0:
```python
import jax
import jax.numpy as jnp
from jax import lax
from jax.sharding import Mesh
from jax.sharding import PartitionSpec as P

EXPERTS = 32
TOP = 8
CAP = 12
HEAD = ("head_0", "head_1")
eps_value = 1e-05


def cut_along(x, dim, count):
    shape = x.shape
    pieces = x.reshape(*shape[:dim], count, shape[dim] // count, *shape[dim + 1 :])
    return jnp.moveaxis(pieces, dim, 0)


def sum_at_owner(x, axis, dim):
    pieces = cut_along(x, dim, lax.axis_size(axis))
    arrived = lax.all_to_all(pieces, axis, split_axis=0, concat_axis=0, tiled=True)
    return arrived.astype(jnp.float32).sum(axis=0)


def over_axes(x, axes):
    for axis in axes:
        x = lax.psum(x, axis)
    return x


def gather_axes(x, axes, dim):
    result = x
    for number in range(len(axes) - 1, -1, -1):
        result = lax.all_gather(result, axes[number], axis=dim, tiled=True)
    return result


def on_device(
    context, out_proj, stream, norm_gain, expert_ids, slot_ids, gate_probs, w_gate, w_up, w_down
):
    local_context = context[0]
    own_stream = stream[0]
    col_width = own_stream.shape[1]
    full_width = col_width * lax.axis_size(HEAD)
    col_start = lax.axis_index(HEAD) * col_width
    partial_value = jnp.dot(
        local_context,
        lax.all_gather(out_proj, "exp", axis=1, tiled=True),
        preferred_element_type=jnp.float32,
    )
    resid_own = sum_at_owner(partial_value.astype(jnp.bfloat16), HEAD, 1) + own_stream
    total_sq = over_axes(jnp.sum(resid_own * resid_own, axis=1, keepdims=True), HEAD)
    gain_own = lax.dynamic_slice_in_dim(norm_gain, col_start, col_width, 0)
    normed_own = (resid_own * lax.rsqrt(total_sq / full_width + eps_value) * gain_own).astype(
        jnp.bfloat16
    )
    choice_ids = expert_ids[0]
    choice_slots = slot_ids[0]
    weights = gate_probs[0]
    spill_slot = EXPERTS * CAP
    target = jnp.where(choice_slots >= 0, choice_ids * CAP + choice_slots, spill_slot)
    outgoing = (
        jnp.zeros((spill_slot + 1, col_width), jnp.bfloat16)
        .at[target.reshape(-1)]
        .set(jnp.repeat(normed_own, TOP, axis=0))
    )
    outgoing = outgoing[:spill_slot].reshape(EXPERTS, CAP, col_width)
    tok_count = lax.axis_size("tok")
    groups = tok_count * lax.axis_size("exp")
    local_experts = w_gate.shape[0]
    arrived = lax.all_to_all(outgoing, ("tok", "exp"), split_axis=0, concat_axis=0, tiled=True)
    arrived = arrived.reshape(groups, local_experts, CAP, col_width)
    piece = gather_axes(arrived, HEAD, 3)
    gate_more = jnp.einsum("slcd,lhd->slch", piece, w_gate, preferred_element_type=jnp.float32)
    up_more = jnp.einsum("slcd,lhd->slch", piece, w_up, preferred_element_type=jnp.float32)
    hidden = (jax.nn.silu(gate_more) * up_more).astype(jnp.bfloat16)
    produced = jnp.einsum(
        "slch,lhd->slcd", hidden, w_down, preferred_element_type=jnp.float32
    ).astype(jnp.bfloat16)
    widened = lax.optimization_barrier(produced).astype(jnp.float32)
    summed = sum_at_owner(widened.astype(jnp.bfloat16), HEAD, 3)
    returned_share = lax.all_to_all(
        summed.reshape(EXPERTS, CAP, col_width).astype(jnp.bfloat16),
        ("tok", "exp"),
        split_axis=0,
        concat_axis=0,
        tiled=True,
    ).astype(jnp.float32)
    lookup_share = jnp.concatenate(
        [returned_share.reshape(spill_slot, col_width), jnp.zeros((1, col_width), jnp.float32)],
        axis=0,
    )
    picked_share = lookup_share[target]
    expert_own = jnp.sum(picked_share * weights[:, :, None], axis=1)
    return (resid_own + expert_own)[None]


def solution(mesh):
    split = Mesh(
        mesh.devices.reshape(mesh.shape["tok"], 4, 4, mesh.shape["exp"]),
        ("tok", "head_0", "head_1", "exp"),
    )
    in_specs = (
        P("exp", "tok", HEAD),
        P(HEAD, "exp"),
        P("exp", "tok", HEAD),
        P(),
        P("exp", "tok", None),
        P("exp", "tok", None),
        P("exp", "tok", None),
        P(("tok", "exp"), HEAD, None),
        P(("tok", "exp"), HEAD, None),
        P(("tok", "exp"), HEAD, None),
    )
    out_specs = P("exp", "tok", HEAD)
    return jax.shard_map(
        on_device, mesh=split, in_specs=in_specs, out_specs=out_specs, check_vma=False
    )
```

profile of v0, /device:TPU:1, one launch (start us, length us, event | category | flops | bytes accessed | tf_op | source)
XLA Modules:
  0.0 316.5 jit_solution(14243525346558986769)
XLA Ops:
  6.5 0.0 copy-start
  6.5 0.0 copy-start.4
  6.5 0.0 copy-start.3
  6.5 0.0 copy-start.1
  6.5 0.0 all-gather.5.cloned.1.call-start
  6.6 0.7 all-gather.5.cloned.1.call-update
  7.3 76.2 %all-gather.5.cloned.1.call-done = bf16[256,4096]{1,0:T(8,128)(2,1)} async-done(((bf16[256,256]{1,0:T(8,128)(2,1)}), bf16[256,4096]{1,0:T(8,128)(2,1)}) %all-gather.5.cloned.1.call-update) | async-done | bytes 2097168 | tf_op jit(solution)/shard_map/all_gather | solution.py:49
  83.5 2.1 convolution_convert_fusion.1
  85.6 0.7 copy.38
  86.3 6.5 %all-to-all-start = ((bf16[16,32,256]{2,1,0:T(8,128)(2,1)}), bf16[16,32,256]{2,1,0:T(8,128)(2,1)S(1)}, u32[]{:S(2)}, u32[]{:S(2)}) async-start(bf16[16,32,256]{2,1,0:T(8,128)(2,1)} %bitcast.101), calls=%async_computation | async-start | bytes 524288 | tf_op jit(solution)/shard_map/all_to_all | solution.py:22
  92.8 0.0 all-gather.7.cloned.1.call-start
  92.9 0.0 copy-done.4
  92.9 0.0 copy-done.3
  92.9 0.1 copy.25
  93.0 0.1 select_n.49
  93.1 0.8 dynamic_slice.3
  93.9 6.5 %all-to-all-done = bf16[16,32,256]{2,1,0:T(8,128)(2,1)S(1)} async-done(((bf16[16,32,256]{2,1,0:T(8,128)(2,1)}), bf16[16,32,256]{2,1,0:T(8,128)(2,1)S(1)}, u32[]{:S(2)}, u32[]{:S(2)}) %all-to-all-start) | async-done | bytes 262176 | tf_op jit(solution)/shard_map/all_to_all | solution.py:22
  100.4 0.0 copy-done.1
  100.4 0.1 multiply_reduce_fusion
  100.5 6.6 %psum.14 = f32[32,1]{0,1:T(1,128)S(1)} all-reduce(f32[32,1]{0,1:T(1,128)S(1)} %bitcast.107), channel_id=1, replica_groups=mesh['tok'=2,'head_0'=4,'head_1'=4,'exp'=16] {'head_0'}, use_global_device_ids=true, to_apply=%region_2.0 | all-reduce | flops 32 | bytes 256 | tf_op jit(solution)/shard_map/psum | solution.py:28
  107.1 7.0 %psum.15 = f32[32,1]{0,1:T(1,128)S(1)} all-reduce(f32[32,1]{0,1:T(1,128)S(1)} %psum.14), channel_id=1, replica_groups=mesh['tok'=2,'head_0'=4,'head_1'=4,'exp'=16] {'head_1'}, use_global_device_ids=true, to_apply=%region_3.0 | all-reduce | flops 32 | bytes 256 | tf_op jit(solution)/shard_map/psum | solution.py:28
  114.1 0.1 multiply_convert_fusion
  114.2 1.5 scatter_custom_fusion
  115.8 0.0 copy-start.5
  115.8 44.8 %all_to_all.20 = bf16[32,12,256]{2,1,0:T(8,128)(2,1)S(1)} all-to-all(bf16[32,12,256]{2,1,0:T(8,128)(2,1)S(1)} %reshape.147), channel_id=1, replica_groups=mesh['tok'=2,'head_0'=4,'head_1'=4,'exp'=16] {'tok','exp'}, dimensions={0} | all-to-all | bytes 393216 | tf_op jit(solution)/shard_map/all_to_all | solution.py:72
  160.6 0.1 copy.26
  160.6 13.4 %all-gather = bf16[32,12,1024]{2,0,1:T(8,128)(2,1)} all-gather(bf16[32,12,256]{2,0,1:T(8,128)(2,1)S(1)} %copy.26), channel_id=2, replica_groups=mesh['tok'=2,'head_0'=4,'head_1'=4,'exp'=16] {'head_1'}, dimensions={2}, use_global_device_ids=true | all-gather | bytes 983040 | tf_op jit(solution)/shard_map/all_gather | solution.py:35
  174.0 0.0 all-gather.7.cloned.1.call-update
  174.0 36.9 %all-gather.7.cloned.1.call-done = bf16[32,12,4096]{2,0,1:T(8,128)(2,1)} async-done(((bf16[32,12,1024]{2,0,1:T(8,128)(2,1)}), bf16[32,12,4096]{2,0,1:T(8,128)(2,1)}) %all-gather.7.cloned.1.call-update) | async-done | bytes 3145744 | tf_op jit(solution)/shard_map/all_gather | solution.py:35
  210.9 0.0 copy-done.5
  210.9 3.7 %fusion.6 = f32[32,1,12,192]{3,0,2,1:T(8,128)} fusion(bf16[32,12,4096]{2,0,1:T(8,128)(2,1)} %all-gather.7.cloned.1.call-done, bf16[1,192,4096]{2,1,0:T(8,128)(2,1)S(1)} %copy-done.5), kind=kOutput, calls=%fused_computation.11 | convolution fusion | flops 603979776 | bytes 5013504 | tf_op jit(solution)/shard_map/slcd,lhd->slch/dot_general | solution.py:75
  214.6 0.0 copy-done
  214.6 7.6 %fusion = bf16[32,1,12,4096]{3,0,2,1:T(8,128)(2,1)} fusion(bf16[1,192,4096]{2,1,0:T(8,128)(2,1)S(1)} %copy-done, bf16[32,12,4096]{2,0,1:T(8,128)(2,1)} %all-gather.7.cloned.1.call-done, bf16[1,192,4096]{2,1,0:T(8,128)(2,1)} %param.18, f32[32,1,12,192]{3,0,2,1:T(8,128)} %fusion.6), kind=kOutput, calls=%fused_computation.3 | convolution fusion | flops 1209974784 | bytes 9732096 | tf_op jit(solution)/shard_map/slch,lhd->slcd/dot_general | solution.py:78
  222.2 2.3 copy.37
  224.5 44.0 %all_to_all.21 = bf16[16,32,1,12,256]{4,1,3,2,0:T(8,128)(2,1)} all-to-all(bf16[16,32,1,12,256]{4,1,3,2,0:T(8,128)(2,1)S(1)} %bitcast.102), channel_id=1, replica_groups=mesh['tok'=2,'head_0'=4,'head_1'=4,'exp'=16] {'head_0','head_1'}, dimensions={0} | all-to-all | bytes 6291456 | tf_op jit(solution)/shard_map/all_to_all | solution.py:22
  268.5 0.0 copy-start.2
  268.5 2.6 reduce_sum.46
  271.0 0.8 copy.29
  271.8 14.3 %all-to-all-start.3 = ((bf16[32,12,256]{2,1,0:T(8,128)(2,1)}), bf16[32,12,256]{2,1,0:T(8,128)(2,1)S(1)}, u32[]{:S(2)}, u32[]{:S(2)}) async-start(bf16[32,12,256]{2,1,0:T(8,128)(2,1)} %copy.29), calls=%async_computation.3 | async-start | bytes 524288 | tf_op jit(solution)/shard_map/all_to_all | solution.py:83
  286.2 0.1 copy.30
  286.2 0.1 reshape.158
  286.3 0.0 copy-done.2
  286.3 0.1 copy.31
  286.4 21.4 %all-to-all-done.3 = bf16[32,12,256]{2,1,0:T(8,128)(2,1)S(1)} async-done(((bf16[32,12,256]{2,1,0:T(8,128)(2,1)}), bf16[32,12,256]{2,1,0:T(8,128)(2,1)S(1)}, u32[]{:S(2)}, u32[]{:S(2)}) %all-to-all-start.3) | async-done | bytes 196640 | tf_op jit(solution)/shard_map/all_to_all | solution.py:83
  307.9 1.0 gather_fusion
  308.9 0.1 fusion.28
  309.0 0.6 bitcast_add_fusion
  (9 shorter events, 0.2 us)
Async XLA Ops:
  6.5 208.1 %copy-start = (bf16[1,192,4096]{2,1,0:T(8,128)(2,1)S(1)}, bf16[1,192,4096]{2,1,0:T(8,128)(2,1)}, u32[]{:S(2)}) copy-start(bf16[1,192,4096]{2,1,0:T(8,128)(2,1)} %param.19) | copy-start | bytes 4718596
  6.5 86.4 %copy-start.4 = (s32[1,32,8]{1,2,0:T(8,128)S(1)}, s32[1,32,8]{1,2,0:T(8,128)}, u32[]{:S(2)}) copy-start(s32[1,32,8]{1,2,0:T(8,128)} %param.14) | copy-start | bytes 3076
  6.5 86.4 %copy-start.3 = (s32[1,32,8]{1,2,0:T(8,128)S(1)}, s32[1,32,8]{1,2,0:T(8,128)}, u32[]{:S(2)}) copy-start(s32[1,32,8]{1,2,0:T(8,128)} %param.15) | copy-start | bytes 3076
  6.5 93.9 %copy-start.1 = (f32[1,32,256]{2,1,0:T(8,128)S(1)}, f32[1,32,256]{2,1,0:T(8,128)}, u32[]{:S(2)}) copy-start(f32[1,32,256]{2,1,0:T(8,128)} %param.12) | copy-start | bytes 98308
  6.5 77.0 %all-gather.5.cloned.1.call-start = ((), (), s32[]{:S(2)}) async-start(), calls=%async_computation.4 | async-start | bytes 2228224 | tf_op jit(solution)/shard_map/all_gather | solution.py:49
  86.3 14.1 %all-to-all-start = ((bf16[16,32,256]{2,1,0:T(8,128)(2,1)}), bf16[16,32,256]{2,1,0:T(8,128)(2,1)S(1)}, u32[]{:S(2)}, u32[]{:S(2)}) async-start(bf16[16,32,256]{2,1,0:T(8,128)(2,1)} %bitcast.101), calls=%async_computation | async-start | bytes 524288 | tf_op jit(solution)/shard_map/all_to_all | solution.py:22
  92.8 118.1 %all-gather.7.cloned.1.call-start = ((), (), s32[]{:S(2)}) async-start(), calls=%async_computation.5 | async-start | bytes 3932160 | tf_op jit(solution)/shard_map/all_gather | solution.py:35
  115.8 95.2 %copy-start.5 = (bf16[1,192,4096]{2,1,0:T(8,128)(2,1)S(1)}, bf16[1,192,4096]{2,1,0:T(8,128)(2,1)}, u32[]{:S(2)}) copy-start(bf16[1,192,4096]{2,1,0:T(8,128)(2,1)} %param.17) | copy-start | bytes 4718596
  268.5 17.9 %copy-start.2 = (f32[1,32,8]{1,2,0:T(8,128)S(1)}, f32[1,32,8]{1,2,0:T(8,128)}, u32[]{:S(2)}) copy-start(f32[1,32,8]{1,2,0:T(8,128)} %param.16) | copy-start | bytes 3076
  271.8 36.0 %all-to-all-start.3 = ((bf16[32,12,256]{2,1,0:T(8,128)(2,1)}), bf16[32,12,256]{2,1,0:T(8,128)(2,1)S(1)}, u32[]{:S(2)}, u32[]{:S(2)}) async-start(bf16[32,12,256]{2,1,0:T(8,128)(2,1)} %copy.29), calls=%async_computation.3 | async-start | bytes 524288 | tf_op jit(solution)/shard_map/all_to_all | solution.py:83
Sparse Core Ops, SparseCore 0:
  9.4 74.0 all-gather.4
  174.2 36.7 all-gather.6
where the time goes:
time: 317 us; the launch traced here: 316 us
  waiting for transfers between devices  142 us (45%)
  blocking collectives  116 us (37%)
  starting transfers between devices  20.9 us (7%)
  between operations  13.6 us (4%)
  matrix products  13.3 us (4%)
  local copies, waits for them, and re-layouts  7.68 us (2%)
  other arithmetic  3.61 us (1%)
    all_gather x1, waiting for transfers between devices, on_device(): lax.all_gather(out_proj, 'exp', axis=1, tiled=True)  76.2 us
    all_to_all x1, blocking collectives, on_device(): lax.all_to_all(outgoing, ('tok', 'exp'), split_axis=0, concat_axis=0, til...  44.8 us
    all_to_all x1, blocking collectives, sum_at_owner(): lax.all_to_all(pieces, axis, split_axis=0, concat_axis=0, tiled=True)  44 us
    all_gather x1, waiting for transfers between devices, gather_axes(): result = lax.all_gather(result, axes[number], axis=dim, tiled=True)  36.9 us
    all_to_all x1, waiting for transfers between devices, on_device(): lax.all_to_all(summed.reshape(EXPERTS, CAP, col_width).astype(jnp.bfloat1...  21.4 us
    all_to_all x1, starting transfers between devices, on_device(): lax.all_to_all(summed.reshape(EXPERTS, CAP, col_width).astype(jnp.bfloat1...  14.3 us
    psum x2, blocking collectives, over_axes(): x = lax.psum(x, axis)  13.5 us
    all_gather x1, blocking collectives, gather_axes(): result = lax.all_gather(result, axes[number], axis=dim, tiled=True)  13.4 us
  transfers between devices with their start and end apart: 4, of which 4 were waited for; matrix products, arithmetic and copies ran while one was open for 0% of the time, Pallas kernels for 0%

commit v1 on v0

--- a/solution.py
+++ b/solution.py
@@ -46,7 +46,9 @@
     col_start = lax.axis_index(HEAD) * col_width
     partial_value = jnp.dot(
         local_context,
-        lax.all_gather(out_proj, "exp", axis=1, tiled=True),
+        jnp.concatenate(
+            lax.all_to_all(jnp.stack([out_proj] * lax.axis_size("exp")), "exp", 0, 0), axis=1
+        ),
         preferred_element_type=jnp.float32,
     )
     resid_own = sum_at_owner(partial_value.astype(jnp.bfloat16), HEAD, 1) + own_stream

time: 317 us -> 342 us (1.079)
  blocking collectives: 116 us -> 217 us
  waiting for transfers between devices: 142 us -> 64.8 us
    all_to_all x0 -> x1, blocking collectives: none -> 106 us  [on_device(): lax.all_to_all(jnp.stack([out_proj] * lax.axis_size('exp')), 'exp', 0, 0)]
    all_gather x1 -> x0, waiting for transfers between devices: 76.2 us -> none  [on_device(): lax.all_gather(out_proj, 'exp', axis=1, tiled=True)]
    all_to_all x1, blocking collectives: 44.8 us -> 39.8 us  [on_device(): lax.all_to_all(outgoing, ('tok', 'exp'), split_axis=0, concat_axis=0, til...]
  transfers between devices with their start and end apart: 4 -> 3, of which waited for: 4 -> 3; matrix products, arithmetic and copies ran while one was open for 0% -> 0% of each run, Pallas kernels for 0% -> 0%
where the time goes in v1:
time: 342 us; the launch traced here: 341 us
  blocking collectives  217 us (63%)
  waiting for transfers between devices  64.8 us (19%)
  starting transfers between devices  21.1 us (6%)
  between operations  13.6 us (4%)
  matrix products  11.9 us (3%)
  local copies, waits for them, and re-layouts  9.01 us (3%)
  other arithmetic  3.61 us (1%)
    all_to_all x1, blocking collectives, on_device(): lax.all_to_all(jnp.stack([out_proj] * lax.axis_size('exp')), 'exp', 0, 0)  106 us
    all_to_all x1, blocking collectives, sum_at_owner(): lax.all_to_all(pieces, axis, split_axis=0, concat_axis=0, tiled=True)  44 us
    all_to_all x1, blocking collectives, on_device(): lax.all_to_all(outgoing, ('tok', 'exp'), split_axis=0, concat_axis=0, til...  39.8 us
    all_gather x1, waiting for transfers between devices, gather_axes(): result = lax.all_gather(result, axes[number], axis=dim, tiled=True)  36.9 us
    all_to_all x1, waiting for transfers between devices, on_device(): lax.all_to_all(summed.reshape(EXPERTS, CAP, col_width).astype(jnp.bfloat1...  21.4 us
    all_to_all x1, starting transfers between devices, on_device(): lax.all_to_all(summed.reshape(EXPERTS, CAP, col_width).astype(jnp.bfloat1...  14.3 us
    psum x2, blocking collectives, over_axes(): x = lax.psum(x, axis)  14 us
    all_gather x1, blocking collectives, gather_axes(): result = lax.all_gather(result, axes[number], axis=dim, tiled=True)  13.4 us
  transfers between devices with their start and end apart: 3, of which 3 were waited for; matrix products, arithmetic and copies ran while one was open for 0% of the time, Pallas kernels for 0%

profile of v1, /device:TPU:1, one launch (start us, length us, event | category | flops | bytes accessed | tf_op | source)
XLA Modules:
  0.0 341.1 jit_solution(10242948599187341488)
XLA Ops:
  6.5 0.0 copy-start
  6.5 1.1 copy.26
  7.7 0.2 stack.2
  7.9 0.0 copy-start.2
  7.9 105.8 %all_to_all.25 = bf16[16,256,256]{1,2,0:T(8,128)(2,1)S(1)} all-to-all(bf16[16,256,256]{1,2,0:T(8,128)(2,1)S(1)} %stack.2), channel_id=1, replica_groups=mesh['tok'=2,'head_0'=4,'head_1'=4,'exp'=16] {'exp'}, dimensions={0} | all-to-all | bytes 4194304 | tf_op jit(solution)/shard_map/all_to_all | solution.py:50
  113.7 0.0 copy-start.4
  113.7 0.0 copy-start.5
  113.7 0.0 copy-start.1
  113.7 0.0 copy-done.2
  113.7 0.7 convolution_convert_fusion.1
  114.4 0.7 copy.41
  115.1 6.8 %all-to-all-start.1 = ((bf16[16,32,256]{2,1,0:T(8,128)(2,1)}), bf16[16,32,256]{2,1,0:T(8,128)(2,1)S(1)}, u32[]{:S(2)}, u32[]{:S(2)}) async-start(bf16[16,32,256]{2,1,0:T(8,128)(2,1)} %bitcast.104), calls=%async_computation.1 | async-start | bytes 524288 | tf_op jit(solution)/shard_map/all_to_all | solution.py:22
  121.9 0.0 all-gather.4.cloned.1.call-start
  121.9 0.0 copy-done.4
  122.0 0.0 copy-done.5
  122.0 0.1 copy.28
  122.1 0.1 select_n.49
  122.2 0.8 dynamic_slice.3
  122.9 6.5 %all-to-all-done.1 = bf16[16,32,256]{2,1,0:T(8,128)(2,1)S(1)} async-done(((bf16[16,32,256]{2,1,0:T(8,128)(2,1)}), bf16[16,32,256]{2,1,0:T(8,128)(2,1)S(1)}, u32[]{:S(2)}, u32[]{:S(2)}) %all-to-all-start.1) | async-done | bytes 262176 | tf_op jit(solution)/shard_map/all_to_all | solution.py:22
  129.5 0.0 copy-done.1
  129.5 0.1 multiply_reduce_fusion
  129.6 7.3 %psum.14 = f32[32,1]{0,1:T(1,128)S(1)} all-reduce(f32[32,1]{0,1:T(1,128)S(1)} %bitcast.111), channel_id=1, replica_groups=mesh['tok'=2,'head_0'=4,'head_1'=4,'exp'=16] {'head_0'}, use_global_device_ids=true, to_apply=%region_2.0 | all-reduce | flops 32 | bytes 256 | tf_op jit(solution)/shard_map/psum | solution.py:28
  136.9 6.7 %psum.15 = f32[32,1]{0,1:T(1,128)S(1)} all-reduce(f32[32,1]{0,1:T(1,128)S(1)} %psum.14), channel_id=1, replica_groups=mesh['tok'=2,'head_0'=4,'head_1'=4,'exp'=16] {'head_1'}, use_global_device_ids=true, to_apply=%region_3.0 | all-reduce | flops 32 | bytes 256 | tf_op jit(solution)/shard_map/psum | solution.py:28
  143.7 0.1 multiply_convert_fusion
  143.7 1.5 scatter_custom_fusion
  145.3 0.0 copy-start.6
  145.3 39.8 %all_to_all.26 = bf16[32,12,256]{2,1,0:T(8,128)(2,1)S(1)} all-to-all(bf16[32,12,256]{2,1,0:T(8,128)(2,1)S(1)} %reshape.157), channel_id=1, replica_groups=mesh['tok'=2,'head_0'=4,'head_1'=4,'exp'=16] {'tok','exp'}, dimensions={0} | all-to-all | bytes 393216 | tf_op jit(solution)/shard_map/all_to_all | solution.py:74
  185.2 0.1 copy.29
  185.2 13.4 %all-gather = bf16[32,12,1024]{2,0,1:T(8,128)(2,1)} all-gather(bf16[32,12,256]{2,0,1:T(8,128)(2,1)S(1)} %copy.29), channel_id=2, replica_groups=mesh['tok'=2,'head_0'=4,'head_1'=4,'exp'=16] {'head_1'}, dimensions={2}, use_global_device_ids=true | all-gather | bytes 983040 | tf_op jit(solution)/shard_map/all_gather | solution.py:35
  198.6 0.0 all-gather.4.cloned.1.call-update
  198.6 36.9 %all-gather.4.cloned.1.call-done = bf16[32,12,4096]{2,0,1:T(8,128)(2,1)} async-done(((bf16[32,12,1024]{2,0,1:T(8,128)(2,1)}), bf16[32,12,4096]{2,0,1:T(8,128)(2,1)}) %all-gather.4.cloned.1.call-update) | async-done | bytes 3145744 | tf_op jit(solution)/shard_map/all_gather | solution.py:35
  235.5 0.0 copy-done.6
  235.6 3.7 %fusion.6 = f32[32,1,12,192]{3,0,2,1:T(8,128)} fusion(bf16[32,12,4096]{2,0,1:T(8,128)(2,1)} %all-gather.4.cloned.1.call-done, bf16[1,192,4096]{2,1,0:T(8,128)(2,1)S(1)} %copy-done.6), kind=kOutput, calls=%fused_computation.11 | convolution fusion | flops 603979776 | bytes 5013504 | tf_op jit(solution)/shard_map/slcd,lhd->slch/dot_general | solution.py:77
  239.2 0.0 copy-done
  239.2 7.6 %fusion = bf16[32,1,12,4096]{3,0,2,1:T(8,128)(2,1)} fusion(bf16[1,192,4096]{2,1,0:T(8,128)(2,1)S(1)} %copy-done, bf16[32,12,4096]{2,0,1:T(8,128)(2,1)} %all-gather.4.cloned.1.call-done, bf16[1,192,4096]{2,1,0:T(8,128)(2,1)} %param.18, f32[32,1,12,192]{3,0,2,1:T(8,128)} %fusion.6), kind=kOutput, calls=%fused_computation.3 | convolution fusion | flops 1209974784 | bytes 9732096 | tf_op jit(solution)/shard_map/slch,lhd->slcd/dot_general | solution.py:80
  246.8 2.3 copy.40
  249.1 44.0 %all_to_all.27 = bf16[16,32,1,12,256]{4,1,3,2,0:T(8,128)(2,1)} all-to-all(bf16[16,32,1,12,256]{4,1,3,2,0:T(8,128)(2,1)S(1)} %bitcast.105), channel_id=1, replica_groups=mesh['tok'=2,'head_0'=4,'head_1'=4,'exp'=16] {'head_0','head_1'}, dimensions={0} | all-to-all | bytes 6291456 | tf_op jit(solution)/shard_map/all_to_all | solution.py:22
  293.1 0.0 copy-start.3
  293.1 2.6 reduce_sum.46
  295.6 0.8 copy.32
  296.4 14.3 %all-to-all-start.4 = ((bf16[32,12,256]{2,1,0:T(8,128)(2,1)}), bf16[32,12,256]{2,1,0:T(8,128)(2,1)S(1)}, u32[]{:S(2)}, u32[]{:S(2)}) async-start(bf16[32,12,256]{2,1,0:T(8,128)(2,1)} %copy.32), calls=%async_computation.4 | async-start | bytes 524288 | tf_op jit(solution)/shard_map/all_to_all | solution.py:85
  310.8 0.1 copy.33
  310.9 0.1 reshape.168
  310.9 0.0 copy-done.3
  311.0 0.1 copy.34
  311.0 21.4 %all-to-all-done.4 = bf16[32,12,256]{2,1,0:T(8,128)(2,1)S(1)} async-done(((bf16[32,12,256]{2,1,0:T(8,128)(2,1)}), bf16[32,12,256]{2,1,0:T(8,128)(2,1)S(1)}, u32[]{:S(2)}, u32[]{:S(2)}) %all-to-all-start.4) | async-done | bytes 196640 | tf_op jit(solution)/shard_map/all_to_all | solution.py:85
  332.5 1.0 gather_fusion
  333.5 0.1 fusion.28
  333.7 0.6 bitcast_add_fusion
  (9 shorter events, 0.2 us)
Async XLA Ops:
  6.5 232.7 %copy-start = (bf16[1,192,4096]{2,1,0:T(8,128)(2,1)S(1)}, bf16[1,192,4096]{2,1,0:T(8,128)(2,1)}, u32[]{:S(2)}) copy-start(bf16[1,192,4096]{2,1,0:T(8,128)(2,1)} %param.19) | copy-start | bytes 4718596
  7.9 105.8 %copy-start.2 = (bf16[1,32,256]{2,1,0:T(8,128)(2,1)S(1)}, bf16[1,32,256]{2,1,0:T(8,128)(2,1)}, u32[]{:S(2)}) copy-start(bf16[1,32,256]{2,1,0:T(8,128)(2,1)} %param.10) | copy-start | bytes 49156
  113.7 8.3 %copy-start.4 = (s32[1,32,8]{1,2,0:T(8,128)S(1)}, s32[1,32,8]{1,2,0:T(8,128)}, u32[]{:S(2)}) copy-start(s32[1,32,8]{1,2,0:T(8,128)} %param.15) | copy-start | bytes 3076
  113.7 8.3 %copy-start.5 = (s32[1,32,8]{1,2,0:T(8,128)S(1)}, s32[1,32,8]{1,2,0:T(8,128)}, u32[]{:S(2)}) copy-start(s32[1,32,8]{1,2,0:T(8,128)} %param.14) | copy-start | bytes 3076
  113.7 15.8 %copy-start.1 = (f32[1,32,256]{2,1,0:T(8,128)S(1)}, f32[1,32,256]{2,1,0:T(8,128)}, u32[]{:S(2)}) copy-start(f32[1,32,256]{2,1,0:T(8,128)} %param.12) | copy-start | bytes 98308
  115.1 14.3 %all-to-all-start.1 = ((bf16[16,32,256]{2,1,0:T(8,128)(2,1)}), bf16[16,32,256]{2,1,0:T(8,128)(2,1)S(1)}, u32[]{:S(2)}, u32[]{:S(2)}) async-start(bf16[16,32,256]{2,1,0:T(8,128)(2,1)} %bitcast.104), calls=%async_computation.1 | async-start | bytes 524288 | tf_op jit(solution)/shard_map/all_to_all | solution.py:22
  121.9 113.7 %all-gather.4.cloned.1.call-start = ((), (), s32[]{:S(2)}) async-start(), calls=%async_computation.5 | async-start | bytes 3932160 | tf_op jit(solution)/shard_map/all_gather | solution.py:35
  145.3 90.2 %copy-start.6 = (bf16[1,192,4096]{2,1,0:T(8,128)(2,1)S(1)}, bf16[1,192,4096]{2,1,0:T(8,128)(2,1)}, u32[]{:S(2)}) copy-start(bf16[1,192,4096]{2,1,0:T(8,128)(2,1)} %param.17) | copy-start | bytes 4718596
  293.1 17.9 %copy-start.3 = (f32[1,32,8]{1,2,0:T(8,128)S(1)}, f32[1,32,8]{1,2,0:T(8,128)}, u32[]{:S(2)}) copy-start(f32[1,32,8]{1,2,0:T(8,128)} %param.16) | copy-start | bytes 3076
  296.4 36.0 %all-to-all-start.4 = ((bf16[32,12,256]{2,1,0:T(8,128)(2,1)}), bf16[32,12,256]{2,1,0:T(8,128)(2,1)S(1)}, u32[]{:S(2)}, u32[]{:S(2)}) async-start(bf16[32,12,256]{2,1,0:T(8,128)(2,1)} %copy.32), calls=%async_computation.4 | async-start | bytes 524288 | tf_op jit(solution)/shard_map/all_to_all | solution.py:85
Sparse Core Ops, SparseCore 0:
  198.8 36.7 all-gather.3
